TPU v7x, 32 devices: a whole 2x2x4 slice. The times are simulated.
32 devices in a mesh: tile: 16 (over z, y, core), layer: 2 (over x).
Axes of the slice: x: 2, y: 2, z: 4, core: 2. Of those that a mesh axis runs over, the one named last changes fastest.
Arguments:
- ensemble: float32 [64, 8, 8192], P(None, 'layer', 'tile'), may hold values from -6 to 6
- diff_x: float32 [8, 8192], P('layer', 'tile'), may hold values from 0.04 to 0.2
- diff_z: float32 [8, 8192], P('layer', 'tile'), may hold values from 0.04 to 0.2
- cour_x: float32 [8, 8192], P('layer', 'tile'), may hold values from -0.4 to 0.4
- cour_z: float32 [8, 8192], P('layer', 'tile'), may hold values from -0.4 to 0.4
- obs_cell: int32 [4, 512], replicated, may hold values from 0 to 65535
- obs_radius: int32 [4, 512], replicated, may hold values from 2048 to 8192
- obs_value: float32 [4, 512], replicated, may hold values from -6 to 6
- obs_var: float32 [4, 512], replicated, may hold values from 0.1 to 1
Outputs:
- posterior: float32 [64, 8, 8192], P(None, 'layer', 'tile')
Inputs may be any that keep to these rules, and one draw needn't show every extreme that they name: `obs_cell`: cells are drawn independently over the whole grid; two observations may share a cell.
All inputs are finite; a program needn't handle non-finite values.
Results may differ from a plain program's by a relative error of at most 0.00019.
Values sent between devices are 32-bit elements; how exact they have to be, the bound alone decides.
A program may use at most 64 MiB of HBM per device.

v0:
```python
import jax
import jax.numpy as jnp
from jax import lax
from jax.sharding import PartitionSpec as P


def extended(cells, sides, width):
    for axis, dim in sides:
        count = lax.axis_size(axis)
        ends = count - 1
        head = lax.slice_in_dim(cells, 0, width, axis=dim)
        tail = lax.slice_in_dim(cells, cells.shape[dim] - width, cells.shape[dim], axis=dim)
        cells = jnp.concatenate(
            [
                lax.ppermute(tail, axis, [(i, (i + 1) % count) for i in range(ends)]),
                cells,
                lax.ppermute(head, axis, [((i + 1) % count, i) for i in range(ends)]),
            ],
            axis=dim,
        )
    return cells


def increments(prior, value, variance):
    members = prior.shape[1]
    ymean = jnp.mean(prior, axis=1)
    anomaly = prior - ymean[:, None]
    spread = jnp.sum(anomaly * anomaly, axis=1) / (members - 1) + 1e-06
    shrink = variance / (spread + variance)
    postmean = spread * shrink * (ymean / spread + value / variance)
    delta = (postmean - ymean)[:, None] + (jnp.sqrt(shrink) - 1.0)[:, None] * anomaly
    factor = 1.0 / ((members - 1) * spread)
    return (anomaly, delta, factor)


def taper(positions, centres, radius):
    dist = jnp.abs(positions[None, :] - centres[:, None]).astype(jnp.float32)
    frac = jnp.maximum(1.0 - dist / radius[:, None].astype(jnp.float32), 0.0)
    return frac * frac


def pick_local(flat, cells, first_layer, first_col, depth, width, total_cols):
    rows = cells // total_cols - first_layer
    cols = cells % total_cols - first_col
    inside = (rows >= 0) & (rows < depth) & (cols >= 0) & (cols < width)
    index = jnp.where(inside, rows * width + cols, 0)
    values = jnp.take(flat, index, axis=1).T
    return jnp.where(inside[:, None], values, 0.0)


def gather_prior(picked):
    return lax.psum(picked, ("tile", "layer"))


def regress(state, anomaly, delta, weight):
    members, depth, width = state.shape
    count = anomaly.shape[0]
    xmean = jnp.mean(state, axis=0)
    deviation = (state - xmean[None]).reshape(members, depth * width)
    block = min(128, count)
    change = jnp.zeros((members, depth * width), jnp.float32)
    for start in range(0, count, block):
        cov = jnp.dot(anomaly[start : start + block], deviation, precision=lax.Precision.HIGHEST)
        gain = (
            cov.reshape(block, depth, width) * weight[start : start + block][:, None, :]
        ).reshape(block, depth * width)
        change = change + jnp.dot(
            delta[start : start + block].T, gain, precision=lax.Precision.HIGHEST
        )
    return state + change.reshape(members, depth, width)


def shards(ensemble, diff_x, diff_z, cour_x, cour_z, obs_cell, obs_radius, obs_value, obs_var):
    members, depth, width = ensemble.shape
    total_cols = width * lax.axis_size("tile")
    first_col = lax.axis_index("tile") * width
    first_layer = lax.axis_index("layer") * depth
    padded = extended(ensemble, (("tile", 2), ("layer", 1)), 1)
    centre = padded[:, 1:-1, 1:-1]
    upper = padded[:, :-2, 1:-1]
    lower = padded[:, 2:, 1:-1]
    west = padded[:, 1:-1, :-2]
    east = padded[:, 1:-1, 2:]
    state = (
        centre
        + diff_z * (upper - 2.0 * centre + lower)
        + diff_x * (west - 2.0 * centre + east)
        - 0.5 * cour_z * (lower - upper)
        - 0.5 * cour_x * (east - west)
    )
    positions = first_col + jnp.arange(width, dtype=jnp.int32)
    batches, count = obs_cell.shape
    for batch in range(batches):
        cells = obs_cell[batch]
        flat = state.reshape(members, depth * width)
        prior = gather_prior(
            pick_local(flat, cells, first_layer, first_col, depth, width, total_cols)
        )
        anomaly, delta, factor = increments(prior, obs_value[batch], obs_var[batch])
        weight = taper(positions, cells % total_cols, obs_radius[batch]) * factor[:, None]
        state = regress(state, anomaly, delta, weight)
    return state


def solution(mesh):
    in_specs = (
        P(None, "layer", "tile"),
        P("layer", "tile"),
        P("layer", "tile"),
        P("layer", "tile"),
        P("layer", "tile"),
        P(),
        P(),
        P(),
        P(),
    )
    out_specs = P(None, "layer", "tile")
    return jax.shard_map(shards, mesh=mesh, in_specs=in_specs, out_specs=out_specs, check_vma=False)
```

profile of v0, /device:TPU:0, one launch (start us, length us, event | category | flops | bytes accessed | tf_op | source)
XLA Modules:
  0.0 607.9 jit_solution(5944438097676178219)
XLA Ops:
  6.5 1.2 copy.114
  7.9 1.3 collective-permute-start.1
  9.2 3.0 collective-permute-start
  18.0 1.3 collective-permute-start.3
  19.3 4.9 collective-permute-start.2
  24.8 1.1 collective-permute-done.3
  26.0 1.8 collective-permute-done.2
  28.6 1.0 gather_fusion
  30.5 125.8 %all-reduce.5.cloned.1.call-done = f32[512,64]{0,1:T(8,128)} async-done(((f32[512,64]{0,1:T(8,128)}), f32[512,64]{0,1:T(8,128)}) %all-reduce.5.cloned.1.call-update) | async-done | bytes 131088 | tf_op jit(solution)/shard_map/psum | solution.py:52
  156.4 1.0 reduce_sum.108
  158.5 1.0 convolution_multiply_fusion.15
  159.9 1.0 convolution_multiply_fusion.14
  160.9 1.3 copy.123
  162.3 1.0 convolution_multiply_fusion.13
  163.3 1.3 copy.125
  164.6 1.0 convolution_multiply_fusion.12
  165.6 1.3 copy.127
  167.0 1.2 fusion.54
  168.3 1.2 convolution_add_fusion.11
  169.5 1.3 convolution_add_fusion.10
  170.8 1.2 convolution_add_fusion.9
  172.8 1.0 gather_fusion.1
  175.8 121.1 %all-reduce.7.cloned.1.call-done = f32[512,64]{0,1:T(8,128)} async-done(((f32[512,64]{0,1:T(8,128)}), f32[512,64]{0,1:T(8,128)}) %all-reduce.7.cloned.1.call-update) | async-done | bytes 131088 | tf_op jit(solution)/shard_map/psum | solution.py:52
  296.9 1.0 reduce_sum.111
  300.6 1.0 convolution_multiply_fusion.11
  302.0 2.0 convolution_multiply_fusion.10
  303.9 1.3 copy.135
  305.3 1.0 convolution_multiply_fusion.9
  306.3 1.3 copy.137
  307.6 1.0 convolution_multiply_fusion.8
  308.6 1.3 copy.139
  310.0 1.2 fusion.49
  311.3 1.3 convolution_add_fusion.8
  312.5 1.2 convolution_add_fusion.7
  313.8 1.2 convolution_add_fusion.6
  315.8 1.0 gather_fusion.2
  318.6 121.3 %all-reduce.9.cloned.1.call-done = f32[512,64]{0,1:T(8,128)} async-done(((f32[512,64]{0,1:T(8,128)}), f32[512,64]{0,1:T(8,128)}) %all-reduce.9.cloned.1.call-update) | async-done | bytes 131088 | tf_op jit(solution)/shard_map/psum | solution.py:52
  439.9 1.0 reduce_sum.114
  443.5 1.0 convolution_multiply_fusion.7
  444.8 1.0 convolution_multiply_fusion.6
  445.9 1.3 copy.147
  447.2 1.0 convolution_multiply_fusion.5
  448.2 1.3 copy.149
  449.5 1.0 convolution_multiply_fusion.4
  450.6 1.3 copy.151
  452.0 1.2 fusion.44
  453.2 1.2 convolution_add_fusion.5
  454.5 1.3 convolution_add_fusion.4
  455.7 1.2 convolution_add_fusion.3
  457.4 1.2 gather_fusion.3
  460.2 121.6 %all-reduce.11.cloned.1.call-done = f32[512,64]{0,1:T(8,128)} async-done(((f32[512,64]{0,1:T(8,128)}), f32[512,64]{0,1:T(8,128)}) %all-reduce.11.cloned.1.call-update) | async-done | bytes 131088 | tf_op jit(solution)/shard_map/psum | solution.py:52
  581.8 1.0 reduce_sum.117
  585.5 1.0 convolution_multiply_fusion.3
  586.8 2.0 convolution_multiply_fusion.2
  588.8 1.3 copy.159
  590.1 1.0 convolution_multiply_fusion.1
  591.2 1.3 copy.161
  592.5 1.0 convolution_multiply_fusion
  593.5 1.3 copy.163
  594.9 1.2 fusion.39
  596.1 1.3 convolution_add_fusion.2
  597.4 1.2 convolution_add_fusion.1
  598.7 1.2 convolution_add_fusion
  600.0 1.1 copy.165
  (172 shorter events, 25.7 us)
Async XLA Ops:
  6.5 149.8 %all-reduce.5.cloned.1.call-start = ((), (), s32[]{:S(2)}) async-start(), calls=%async_computation | async-start | bytes 262144 | tf_op jit(solution)/shard_map/psum | solution.py:52
  7.8 4.4 copy-start.30
  7.9 10.0 %collective-permute-start.1 = (f32[64,4,1]{2,0,1:T(8,128)S(1)}, f32[64,4,1]{2,0,1:T(8,128)S(1)}, u32[]{:S(2)}, u32[]{:S(2)}) collective-permute-start(f32[64,4,1]{2,0,1:T(8,128)S(1)} %get-tuple-element.53), channel_id=1, source_target_pairs={{2,0},{4,2},{6,4},{8,6},{10,8},{12,10},{14,12},{16,14},{18,16},{20... | collective-permute-start | bytes 3080 | tf_op jit(solution)/shard_map/ppermute | solution.py:17
  9.2 8.7 %collective-permute-start = (f32[64,4,1]{2,0,1:T(8,128)S(1)}, f32[64,4,1]{2,0,1:T(8,128)S(1)}, u32[]{:S(2)}, u32[]{:S(2)}) collective-permute-start(f32[64,4,1]{2,0,1:T(8,128)S(1)} %get-tuple-element.52), channel_id=1, source_target_pairs={{0,2},{2,4},{4,6},{6,8},{8,10},{10,12},{12,14},{14,16},{16,18},{18... | collective-permute-start | bytes 3080 | tf_op jit(solution)/shard_map/ppermute | solution.py:15
  13.9 1.2 copy-start.31
  15.2 0.7 copy-start.32
  15.8 0.7 copy-start.33
  16.5 0.7 copy-start.34
  16.5 0.7 copy-start.35
  18.0 7.9 %collective-permute-start.3 = (f32[64,1,514]{2,0,1:T(8,128)S(1)}, f32[64,1,514]{2,0,1:T(8,128)S(1)}, u32[]{:S(2)}, u32[]{:S(2)}) collective-permute-start(f32[64,1,514]{2,0,1:T(8,128)S(1)} %get-tuple-element.51), channel_id=1, source_target_pairs={{1,0},{3,2},{5,4},{7,6},{9,8},{11,10},{13,12},{15,14},{17,16},{19,... | collective-permute-start | bytes 394760 | tf_op jit(solution)/shard_map/ppermute | solution.py:17
  19.3 8.4 %collective-permute-start.2 = (f32[64,1,514]{2,0,1:T(8,128)S(1)}, f32[64,1,514]{2,0,1:T(8,128)S(1)}, u32[]{:S(2)}, u32[]{:S(2)}) collective-permute-start(f32[64,1,514]{2,0,1:T(8,128)S(1)} %get-tuple-element.50), channel_id=1, source_target_pairs={{0,1},{2,3},{4,5},{6,7},{8,9},{10,11},{12,13},{14,15},{16,17},{18,... | collective-permute-start | bytes 394760 | tf_op jit(solution)/shard_map/ppermute | solution.py:15
  24.2 3.5 copy-start.18
  24.2 3.5 copy-start.19
  30.5 266.4 %all-reduce.7.cloned.1.call-start = ((), (), s32[]{:S(2)}) async-start(), calls=%async_computation.1 | async-start | bytes 262144 | tf_op jit(solution)/shard_map/psum | solution.py:52
  156.4 1.0 copy-start.12
  165.6 1.4 copy-start.20
  165.6 1.4 copy-start.21
  167.0 1.3 copy-start
  168.3 1.3 copy-start.4
  169.5 1.3 copy-start.8
  172.2 0.7 copy-start.17
  174.0 0.6 copy-start.46
  174.0 0.6 copy-start.47
  175.3 264.6 %all-reduce.9.cloned.1.call-start = ((), (), s32[]{:S(2)}) async-start(), calls=%async_computation.2 | async-start | bytes 262144 | tf_op jit(solution)/shard_map/psum | solution.py:52
  296.9 1.0 copy-start.13
  298.0 0.7 copy-start.41
  298.0 0.7 copy-start.40
  298.7 0.7 copy-start.29
  298.7 0.7 copy-start.26
  310.0 1.3 copy-start.1
  311.2 1.3 copy-start.5
  312.5 1.3 copy-start.9
  315.1 0.7 copy-start.16
  317.0 0.7 copy-start.44
  317.0 0.7 copy-start.45
  318.4 263.4 %all-reduce.11.cloned.1.call-start = ((), (), s32[]{:S(2)}) async-start(), calls=%async_computation.3 | async-start | bytes 262144 | tf_op jit(solution)/shard_map/psum | solution.py:52
  439.9 1.0 copy-start.14
  441.0 0.7 copy-start.39
  441.0 0.7 copy-start.38
  442.3 0.7 copy-start.28
  442.3 0.7 copy-start.25
  450.6 1.4 copy-start.22
  450.6 1.4 copy-start.23
  451.9 1.3 copy-start.2
  453.2 1.3 copy-start.6
  454.5 1.3 copy-start.10
  458.8 0.6 copy-start.42
  458.8 0.7 copy-start.43
  581.8 1.0 copy-start.15
  582.9 0.7 copy-start.37
  582.9 0.7 copy-start.36
  583.6 0.7 copy-start.27
  583.6 0.7 copy-start.24
  594.8 1.3 copy-start.3
  596.1 1.3 copy-start.7
  597.4 1.3 copy-start.11
Sparse Core Ops, SparseCore 0:
  30.6 125.7 all-reduce.4
  175.4 121.4 all-reduce.6
  318.5 121.4 all-reduce.8
  460.3 121.4 all-reduce.10
where the time goes:
time: 617 us; the launch traced here: 608 us
  waiting for transfers between devices  493 us (80%)
  matrix products  38.2 us (6%)
  local copies, waits for them, and re-layouts  35.8 us (6%)
  other arithmetic  15.7 us (3%)
  between operations  14.2 us (2%)
  starting transfers between devices  11.2 us (2%)
    psum x4, waiting for transfers between devices, gather_prior(): return lax.psum(picked, ('tile', 'layer'))  490 us
    dot_general x16, matrix products, regress(): jnp.dot(delta[start:start + block].T, gain, precision=lax.Precision.HIGHEST)  20 us
    dot_general x16, matrix products, regress(): jnp.dot(anomaly[start:start + block], deviation, precision=lax.Precision....  18.2 us
    mul x16, local copies, waits for them, and re-layouts, regress(): cov.reshape(block, depth, width) * weight[start:start + block][:, None, :]  17.2 us
  transfers between devices with their start and end apart: 8, of which 6 were waited for; matrix products, arithmetic and copies ran while one was open for 1% of the time, Pallas kernels for 0%

commit v1 on v0

--- a/solution.py
+++ b/solution.py
@@ -1,7 +1,16 @@
+import functools
 import jax
 import jax.numpy as jnp
 from jax import lax
 from jax.sharding import PartitionSpec as P
+from jax.lax import psum
+
+
+def cube_start(obj, comm_axis, ax_name):
+    return psum(psum(obj, axis_name=comm_axis), axis_name=ax_name)
+
+
+start_positions = functools.partial(cube_start, comm_axis="layer", ax_name="tile")
 
 
 def extended(cells, sides, width):
@@ -49,7 +58,7 @@
 
 
 def gather_prior(picked):
-    return lax.psum(picked, ("tile", "layer"))
+    return start_positions(picked)
 
 
 def regress(state, anomaly, delta, weight):

time: 617 us -> 582 us (0.943)
  waiting for transfers between devices: 493 us -> 456 us
    psum x4 -> x8, waiting for transfers between devices: 490 us -> 453 us  [cube_start(): return psum(psum(obj, axis_name=comm_axis), axis_name=ax_name)]
  transfers between devices with their start and end apart: 8 -> 12, of which waited for: 6 -> 10; matrix products, arithmetic and copies ran while one was open for 1% -> 1% of each run, Pallas kernels for 0% -> 0%
where the time goes in v1:
time: 582 us; the launch traced here: 572 us
  waiting for transfers between devices  456 us (78%)
  matrix products  38.2 us (7%)
  local copies, waits for them, and re-layouts  37.4 us (6%)
  between operations  14.6 us (3%)
  other arithmetic  14 us (2%)
  starting transfers between devices  11.6 us (2%)
    psum x8, waiting for transfers between devices, cube_start(): return psum(psum(obj, axis_name=comm_axis), axis_name=ax_name)  453 us
    dot_general x16, matrix products, regress(): jnp.dot(delta[start:start + block].T, gain, precision=lax.Precision.HIGHEST)  20 us
    dot_general x16, matrix products, regress(): jnp.dot(anomaly[start:start + block], deviation, precision=lax.Precision....  18.2 us
    mul x16, local copies, waits for them, and re-layouts, regress(): cov.reshape(block, depth, width) * weight[start:start + block][:, None, :]  17.2 us
  transfers between devices with their start and end apart: 12, of which 10 were waited for; matrix products, arithmetic and copies ran while one was open for 1% of the time, Pallas kernels for 0%

profile of v1, /device:TPU:0, one launch (start us, length us, event | category | flops | bytes accessed | tf_op | source)
XLA Modules:
  0.0 571.5 jit_solution(6593025319970472767)
XLA Ops:
  6.5 1.2 copy.114
  7.9 1.3 collective-permute-start.1
  9.2 3.0 collective-permute-start
  15.8 1.3 collective-permute-start.3
  17.1 4.9 collective-permute-start.2
  22.7 1.1 collective-permute-done.3
  23.7 1.8 collective-permute-done.2
  26.4 1.0 gather_fusion
  28.9 25.1 %all-reduce.9.cloned.1.call-done = f32[512,64]{0,1:T(8,128)} async-done(((f32[512,64]{0,1:T(8,128)}), f32[512,64]{0,1:T(8,128)}) %all-reduce.9.cloned.1.call-update) | async-done | bytes 131088 | tf_op jit(solution)/shard_map/psum | solution.py:10
  54.1 90.3 %all-reduce.11.cloned.1.call-done = f32[512,64]{0,1:T(8,128)} async-done(((f32[512,64]{0,1:T(8,128)}), f32[512,64]{0,1:T(8,128)}) %all-reduce.11.cloned.1.call-update) | async-done | bytes 131088 | tf_op jit(solution)/shard_map/psum | solution.py:10
  146.5 1.0 convolution_multiply_fusion.15
  147.9 1.0 convolution_multiply_fusion.14
  148.9 1.3 copy.123
  150.3 1.0 convolution_multiply_fusion.13
  151.3 1.3 copy.125
  152.6 1.0 convolution_multiply_fusion.12
  153.6 1.3 copy.127
  155.0 1.2 fusion.54
  156.3 1.2 convolution_add_fusion.11
  157.5 1.3 convolution_add_fusion.10
  158.8 1.2 convolution_add_fusion.9
  160.8 1.0 gather_fusion.1
  164.1 22.5 %all-reduce.13.cloned.1.call-done = f32[512,64]{0,1:T(8,128)} async-done(((f32[512,64]{0,1:T(8,128)}), f32[512,64]{0,1:T(8,128)}) %all-reduce.13.cloned.1.call-update) | async-done | bytes 131088 | tf_op jit(solution)/shard_map/psum | solution.py:10
  187.1 89.7 %all-reduce.15.cloned.1.call-done = f32[512,64]{0,1:T(8,128)} async-done(((f32[512,64]{0,1:T(8,128)}), f32[512,64]{0,1:T(8,128)}) %all-reduce.15.cloned.1.call-update) | async-done | bytes 131088 | tf_op jit(solution)/shard_map/psum | solution.py:10
  280.5 1.0 convolution_multiply_fusion.11
  281.8 2.0 convolution_multiply_fusion.10
  283.8 1.3 copy.135
  285.1 1.0 convolution_multiply_fusion.9
  286.2 1.3 copy.137
  287.5 1.0 convolution_multiply_fusion.8
  288.5 1.3 copy.139
  289.8 1.2 fusion.49
  291.1 1.3 convolution_add_fusion.8
  292.4 1.2 convolution_add_fusion.7
  293.6 1.2 convolution_add_fusion.6
  295.3 1.0 gather_fusion.2
  299.1 22.0 %all-reduce.17.cloned.1.call-done = f32[512,64]{0,1:T(8,128)} async-done(((f32[512,64]{0,1:T(8,128)}), f32[512,64]{0,1:T(8,128)}) %all-reduce.17.cloned.1.call-update) | async-done | bytes 131088 | tf_op jit(solution)/shard_map/psum | solution.py:10
  321.3 90.0 %all-reduce.19.cloned.1.call-done = f32[512,64]{0,1:T(8,128)} async-done(((f32[512,64]{0,1:T(8,128)}), f32[512,64]{0,1:T(8,128)}) %all-reduce.19.cloned.1.call-update) | async-done | bytes 131088 | tf_op jit(solution)/shard_map/psum | solution.py:10
  414.8 1.0 convolution_multiply_fusion.7
  416.1 1.0 convolution_multiply_fusion.6
  417.2 1.3 copy.147
  418.5 1.0 convolution_multiply_fusion.5
  419.5 1.3 copy.149
  420.9 1.0 convolution_multiply_fusion.4
  421.9 1.3 copy.151
  423.3 1.2 fusion.44
  424.5 1.2 convolution_add_fusion.5
  425.8 1.3 convolution_add_fusion.4
  427.0 1.2 convolution_add_fusion.3
  429.1 1.0 gather_fusion.3
  431.9 22.9 %all-reduce.21.cloned.1.call-done = f32[512,64]{0,1:T(8,128)} async-done(((f32[512,64]{0,1:T(8,128)}), f32[512,64]{0,1:T(8,128)}) %all-reduce.21.cloned.1.call-update) | async-done | bytes 131088 | tf_op jit(solution)/shard_map/psum | solution.py:10
  454.9 90.3 %all-reduce.23.cloned.1.call-done = f32[512,64]{0,1:T(8,128)} async-done(((f32[512,64]{0,1:T(8,128)}), f32[512,64]{0,1:T(8,128)}) %all-reduce.23.cloned.1.call-update) | async-done | bytes 131088 | tf_op jit(solution)/shard_map/psum | solution.py:10
  548.8 1.0 convolution_multiply_fusion.3
  550.2 2.0 convolution_multiply_fusion.2
  552.2 1.3 copy.159
  553.5 1.0 convolution_multiply_fusion.1
  554.5 1.3 copy.161
  555.8 1.0 convolution_multiply_fusion
  556.9 1.3 copy.163
  558.2 1.2 fusion.39
  559.5 1.3 convolution_add_fusion.2
  560.7 1.2 convolution_add_fusion.1
  562.0 1.2 convolution_add_fusion
  563.3 1.1 copy.165
  (190 shorter events, 30.4 us)
Async XLA Ops:
  6.5 47.5 %all-reduce.9.cloned.1.call-start = ((), (), s32[]{:S(2)}) async-start(), calls=%async_computation | async-start | bytes 262144 | tf_op jit(solution)/shard_map/psum | solution.py:10
  7.8 4.4 copy-start.31
  7.9 7.8 %collective-permute-start.1 = (f32[64,4,1]{2,0,1:T(8,128)S(1)}, f32[64,4,1]{2,0,1:T(8,128)S(1)}, u32[]{:S(2)}, u32[]{:S(2)}) collective-permute-start(f32[64,4,1]{2,0,1:T(8,128)S(1)} %get-tuple-element.53), channel_id=1, source_target_pairs={{2,0},{4,2},{6,4},{8,6},{10,8},{12,10},{14,12},{16,14},{18,16},{20... | collective-permute-start | bytes 3080 | tf_op jit(solution)/shard_map/ppermute | solution.py:26
  9.2 6.5 %collective-permute-start = (f32[64,4,1]{2,0,1:T(8,128)S(1)}, f32[64,4,1]{2,0,1:T(8,128)S(1)}, u32[]{:S(2)}, u32[]{:S(2)}) collective-permute-start(f32[64,4,1]{2,0,1:T(8,128)S(1)} %get-tuple-element.52), channel_id=1, source_target_pairs={{0,2},{2,4},{4,6},{6,8},{8,10},{10,12},{12,14},{14,16},{16,18},{18... | collective-permute-start | bytes 3080 | tf_op jit(solution)/shard_map/ppermute | solution.py:24
  12.2 0.7 copy-start.32
  12.9 0.7 copy-start.33
  13.6 0.7 copy-start.34
  14.3 0.7 copy-start.18
  14.3 7.7 %copy-start.16 = (s32[1,512]{1,0:T(1,128)}, s32[1,512]{1,0:T(1,128)S(1)}, u32[]{:S(2)}) copy-start(s32[1,512]{1,0:T(1,128)S(1)} %get-tuple-element.69) | copy-start | bytes 6148
  14.3 0.7 copy-start.37
  14.3 0.7 copy-start.38
  15.8 7.9 %collective-permute-start.3 = (f32[64,1,514]{2,0,1:T(8,128)S(1)}, f32[64,1,514]{2,0,1:T(8,128)S(1)}, u32[]{:S(2)}, u32[]{:S(2)}) collective-permute-start(f32[64,1,514]{2,0,1:T(8,128)S(1)} %get-tuple-element.51), channel_id=1, source_target_pairs={{1,0},{3,2},{5,4},{7,6},{9,8},{11,10},{13,12},{15,14},{17,16},{19,... | collective-permute-start | bytes 394760 | tf_op jit(solution)/shard_map/ppermute | solution.py:26
  17.1 8.4 %collective-permute-start.2 = (f32[64,1,514]{2,0,1:T(8,128)S(1)}, f32[64,1,514]{2,0,1:T(8,128)S(1)}, u32[]{:S(2)}, u32[]{:S(2)}) collective-permute-start(f32[64,1,514]{2,0,1:T(8,128)S(1)} %get-tuple-element.50), channel_id=1, source_target_pairs={{0,1},{2,3},{4,5},{6,7},{8,9},{10,11},{12,13},{14,15},{16,17},{18,... | collective-permute-start | bytes 394760 | tf_op jit(solution)/shard_map/ppermute | solution.py:24
  22.0 3.5 copy-start.23
  22.7 2.9 copy-start.22
  28.3 116.1 %all-reduce.11.cloned.1.call-start = ((), (), s32[]{:S(2)}) async-start(), calls=%async_computation.1 | async-start | bytes 262144 | tf_op jit(solution)/shard_map/psum | solution.py:10
  54.0 132.6 %all-reduce.13.cloned.1.call-start = ((), (), s32[]{:S(2)}) async-start(), calls=%async_computation.2 | async-start | bytes 262144 | tf_op jit(solution)/shard_map/psum | solution.py:10
  144.4 1.0 copy-start.12
  153.6 1.3 copy-start.24
  153.6 1.3 copy-start.25
  155.0 1.3 copy-start
  156.2 1.3 copy-start.4
  157.5 1.3 copy-start.8
  160.1 0.7 copy-start.20
  162.0 0.6 copy-start.49
  162.0 0.7 copy-start.50
  163.3 0.7 copy-start.19
  163.4 0.7 copy-start.36
  163.4 113.4 %all-reduce.15.cloned.1.call-start = ((), (), s32[]{:S(2)}) async-start(), calls=%async_computation.3 | async-start | bytes 262144 | tf_op jit(solution)/shard_map/psum | solution.py:10
  186.6 134.4 %all-reduce.17.cloned.1.call-start = ((), (), s32[]{:S(2)}) async-start(), calls=%async_computation.4 | async-start | bytes 262144 | tf_op jit(solution)/shard_map/psum | solution.py:10
  276.8 1.0 copy-start.13
  277.9 0.7 copy-start.44
  277.9 0.7 copy-start.43
  278.6 0.7 copy-start.30
  289.8 1.3 copy-start.1
  291.1 1.3 copy-start.5
  292.4 1.3 copy-start.9
  296.5 0.6 copy-start.47
  296.5 0.6 copy-start.48
  297.8 0.7 copy-start.17
  297.8 0.7 copy-start.35
  297.8 113.4 %all-reduce.19.cloned.1.call-start = ((), (), s32[]{:S(2)}) async-start(), calls=%async_computation.5 | async-start | bytes 262144 | tf_op jit(solution)/shard_map/psum | solution.py:10
  321.1 133.8 %all-reduce.21.cloned.1.call-start = ((), (), s32[]{:S(2)}) async-start(), calls=%async_computation.6 | async-start | bytes 262144 | tf_op jit(solution)/shard_map/psum | solution.py:10
  411.3 1.0 copy-start.14
  412.3 0.7 copy-start.42
  412.3 0.7 copy-start.41
  413.6 0.7 copy-start.29
  421.9 1.3 copy-start.26
  421.9 1.3 copy-start.27
  423.2 1.3 copy-start.2
  424.5 1.3 copy-start.6
  425.8 1.3 copy-start.10
  428.4 0.7 copy-start.21
  430.2 0.7 copy-start.45
  430.3 0.7 copy-start.46
  431.6 113.6 %all-reduce.23.cloned.1.call-start = ((), (), s32[]{:S(2)}) async-start(), calls=%async_computation.7 | async-start | bytes 262144 | tf_op jit(solution)/shard_map/psum | solution.py:10
  545.2 1.0 copy-start.15
  546.3 0.7 copy-start.40
  546.3 0.7 copy-start.39
  547.0 0.6 copy-start.28
  558.2 1.3 copy-start.3
  559.5 1.3 copy-start.7
  560.7 1.3 copy-start.11
Sparse Core Ops, SparseCore 0:
  28.4 25.5 all-reduce.8
  57.4 86.8 all-reduce.10
  163.5 23.0 all-reduce.12
  189.9 86.8 all-reduce.14
  297.9 23.0 all-reduce.16
  324.3 86.8 all-reduce.18
  431.7 23.0 all-reduce.20
  458.3 86.8 all-reduce.22
